TPU v7x, 128 devices: a whole 4x4x4 slice. The times are simulated.
128 devices in a mesh: dp: 16 (over x, z), col: 8 (over y, core).
Axes of the slice: x: 4, y: 4, z: 4, core: 2. Of those that a mesh axis runs over, the one named last changes fastest.
Arguments:
- coefficients: bfloat16 [16, 65536], P(None, 'dp'), may hold values from -0.3125 to 0.3125
- arc_pairs: int32 [2, 65536], P(None, 'dp'), may hold values from 0 to 31, as said below
- live_rows: int32 [16], P('dp'), may hold values from 1 to 4096, 32768 in all
- shared_rows: bfloat16 [65536, 16384], P('dp', 'col'), may hold values from -6 to 6
- prior_panel: float32 [256, 256], replicated, as said below
- prior_shared: float32 [256, 16384], P(None, 'col'), may hold values from -4 to 4
Outputs:
- new_panel: float32 [256, 256], replicated
- new_shared: float32 [256, 16384], P(None, 'col')
Inputs may be any that keep to these rules, and one draw needn't show every extreme that they name: `arc_pairs`: the two arcs of a row differ. `prior_panel`: upper triangular with a positive diagonal.
All inputs are finite; a program needn't handle non-finite values. No bound on the sum of `live_rows` on one device may be relied on, other than what follows from the above.
Results may differ from a plain program's by a relative error of at most 0.0003.
Values sent between devices are 32-bit elements; how exact they have to be, the bound alone decides.
A program may use at most 64 MiB of HBM per device.

v0:
```python
import jax
import jax.numpy as jnp
from jax import lax
from jax.sharding import PartitionSpec as P

ARCS = 32


def make_panel(coefficients, arc_pairs, live_mask):
    arc_par = coefficients.shape[0] // 2
    panel_width = ARCS * arc_par
    column_arc = jnp.arange(panel_width, dtype=jnp.int32) // arc_par
    first_coef = jnp.tile(coefficients[:arc_par].T, (1, ARCS))
    second_coef = jnp.tile(coefficients[arc_par:].T, (1, ARCS))
    hit_first = arc_pairs[0][:, None] == column_arc[None, :]
    hit_second = arc_pairs[1][:, None] == column_arc[None, :]
    zero_value = jnp.zeros((), coefficients.dtype)
    panel_rows = jnp.where(hit_first, first_coef, zero_value) + jnp.where(
        hit_second, second_coef, zero_value
    )
    return jnp.where(live_mask[:, None], panel_rows, zero_value)


def row_product(shared_block, panel_rows):
    return lax.dot_general(
        shared_block, panel_rows, (((0,), (0,)), ((), ())), preferred_element_type=jnp.float32
    )


def per_device(coefficients, arc_pairs, live_rows, shared_rows, prior_panel, prior_shared):
    row_count = coefficients.shape[1]
    live_mask = jnp.arange(row_count, dtype=jnp.int32) < live_rows[0]
    panel_rows = make_panel(coefficients, arc_pairs, live_mask)
    prior_gram = jnp.dot(prior_panel.T, prior_panel, precision=lax.Precision.HIGHEST)
    row_share = row_count // lax.axis_size("col")
    own_rows = lax.dynamic_slice_in_dim(panel_rows, lax.axis_index("col") * row_share, row_share, 0)
    gram_data = lax.psum(
        jnp.dot(own_rows.T, own_rows, preferred_element_type=jnp.float32), ("dp", "col")
    )
    cross_local = row_product(shared_rows, panel_rows)
    cross_data = lax.psum(cross_local, "dp")
    factor_lower = jnp.linalg.cholesky(prior_gram + gram_data)
    cross = jnp.dot(prior_panel.T, prior_shared, precision=lax.Precision.HIGHEST) + cross_data.T
    new_shared = lax.linalg.triangular_solve(factor_lower, cross, left_side=True, lower=True)
    return (factor_lower.T, new_shared)


def solution(mesh):
    in_specs = (P(None, "dp"), P(None, "dp"), P("dp"), P("dp", "col"), P(), P(None, "col"))
    out_specs = (P(), P(None, "col"))
    return jax.shard_map(
        per_device, mesh=mesh, in_specs=in_specs, out_specs=out_specs, check_vma=False
    )
```

profile of v0, /device:TPU:0, one launch (start us, length us, event | category | flops | bytes accessed | tf_op | source)
XLA Modules:
  0.0 264.5 jit_solution(13563509152262519315)
XLA Ops:
  7.2 0.0 copy-start
  7.2 0.0 all-reduce.4.cloned.1.call-start
  8.0 0.9 fusion.18
  8.9 0.9 slice_bitcast_fusion.5
  9.8 1.3 fusion.1
  11.1 1.0 fusion.5
  12.1 0.0 all-reduce.4.cloned.1.call-update
  12.1 0.0 all-reduce.6.cloned.1.call-start
  12.2 9.8 %fusion.15 = f32[256,2048]{1,0:T(8,128)} fusion(bf16[4096,2048]{1,0:T(8,128)(2,1)} %param.9, s32[4096]{0:T(1024)S(1)} %bitcast.55, s32[4096]{0:T(1024)S(1)} %bitcast.53, s32[256]{0:T(256)S(1)} %and_select_fusion, pred[4096]{0:T(1024)(128)(4,1)S(1)} %iota_compare_fusion.3, bf16[4096,8]{0,1:T(8,128)(2,1)S(1)} %get-tuple-element.27, ...), kind=kOutput, calls=%fused_computation.46 | convolution fusion | flops 4301258752 | bytes 19043328 | tf_op jit(solution)/shard_map/dot_general | solution.py:25
  22.0 0.0 copy-start.1
  22.0 0.0 all-reduce.6.cloned.1.call-update
  22.0 135.8 %all-reduce.4.cloned.1.call-done = f32[256,256]{0,1:T(8,128)} async-done(((f32[256,256]{0,1:T(8,128)}), f32[256,256]{0,1:T(8,128)}) %all-reduce.4.cloned.1.call-update) | async-done | bytes 262160 | tf_op jit(solution)/shard_map/psum | solution.py:37
  157.8 0.0 copy-done.1
  157.8 1.5 convolution_add_fusion.1
  159.4 0.1 copy.16
  159.6 11.7 %cholesky.50 = f32[128,128]{1,0:T(8,128)S(1)} custom-call(f32[128,128]{1,0:T(8,128)S(1)} %cholesky.118), custom_call_target="Cholesky" | custom-call | tf_op jit(solution)/shard_map/jit(cholesky)/cholesky | solution.py:42
  171.3 9.8 %custom-call.14 = f32[1,128,128]{1,2,0:T(8,128)S(1)} custom-call(f32[1,128,128]{2,1,0:T(8,128)S(1)} %get-tuple-element.31), custom_call_target="InvertDiagBlocksLowerTriangular" | custom-call | tf_op jit(solution)/shard_map/jit(cholesky)/cholesky | solution.py:42
  181.2 0.2 constant_dynamic-update-slice_fusion.1
  181.4 0.3 convolution_subtract_fusion.1
  181.6 11.7 %cholesky.105 = f32[128,128]{1,0:T(8,128)S(1)} custom-call(f32[128,128]{1,0:T(8,128)S(1)} %convolution_subtract_fusion.1), custom_call_target="Cholesky" | custom-call | tf_op jit(solution)/shard_map/jit(cholesky)/cholesky | solution.py:42
  193.4 0.7 compare_reduce_fusion
  195.4 0.8 copy.17
  196.2 0.1 triangular_solve.42
  196.3 3.9 %while.1 = (s32[]{:T(128)}, f32[256,256]{1,0:T(8,128)S(1)}, s32[2,2]{1,0:T(2,128)S(1)}, f32[2,128,128]{2,1,0:T(8,128)S(1)}, s32[]{:T(128)}) while((s32[]{:T(128)}, f32[256,256]{1,0:T(8,128)S(1)}, s32[2,2]{1,0:T(2,128)S(1)}, f32[2,128,128]{2,1,0:T(8,128)S(1)}, s32[]{:T(128)}) %tuple.32), condition=%wide.while_cond, body=%wide.while_body.sunk | while | flops 2 | bytes 131189 | solution.py:44
  196.3 0.6 fusion.29
  196.9 1.3 bitcast_dynamic-update-slice_fusion.2
  198.2 0.6 fusion.29
  198.8 1.3 bitcast_dynamic-update-slice_fusion.2
  200.1 19.9 %custom-call.15 = f32[2,128,128]{1,2,0:T(8,128)S(1)} custom-call(f32[2,128,128]{2,1,0:T(8,128)S(1)} %get-tuple-element.9), custom_call_target="InvertDiagBlocksLowerTriangular" | custom-call | tf_op jit(solution)/shard_map/triangular_solve | solution.py:44
  220.0 29.5 %all-reduce.6.cloned.1.call-done = f32[256,2048]{1,0:T(8,128)} async-done(((f32[256,2048]{1,0:T(8,128)}), f32[256,2048]{1,0:T(8,128)}) %all-reduce.6.cloned.1.call-update) | async-done | bytes 2097168 | tf_op jit(solution)/shard_map/psum | solution.py:41
  249.5 0.0 copy-done
  249.5 3.5 %convolution_add_fusion = f32[256,2048]{1,0:T(8,128)S(1)} fusion(f32[256,2048]{1,0:T(8,128)} %all-reduce.6.cloned.1.call-done, f32[256,256]{1,0:T(8,128)S(1)} %copy-done.1, f32[256,2048]{1,0:T(8,128)S(1)} %copy-done), kind=kOutput, calls=%fused_computation.4 | convolution fusion | flops 1611137024 | bytes 6553600 | tf_op jit(solution)/shard_map/dot_general | solution.py:43
  253.0 1.1 fusion.2
  254.1 1.0 convolution_subtract_fusion
  255.2 1.1 fusion.10
  256.2 1.5 pad_maximum_fusion
  (12 shorter events, 0.2 us)
Async XLA Ops:
  7.2 242.3 %copy-start = (f32[256,2048]{1,0:T(8,128)S(1)}, f32[256,2048]{1,0:T(8,128)}, u32[]{:S(2)}) copy-start(f32[256,2048]{1,0:T(8,128)} %param.11) | copy-start | bytes 6291460
  7.2 150.6 %all-reduce.4.cloned.1.call-start = ((), (), s32[]{:S(2)}) async-start(), calls=%async_computation | async-start | bytes 524288 | tf_op jit(solution)/shard_map/psum | solution.py:37
  12.1 237.3 %all-reduce.6.cloned.1.call-start = ((), (), s32[]{:S(2)}) async-start(), calls=%async_computation.1 | async-start | bytes 4194304 | tf_op jit(solution)/shard_map/psum | solution.py:41
  22.0 135.8 %copy-start.1 = (f32[256,256]{1,0:T(8,128)S(1)}, f32[256,256]{1,0:T(8,128)}, u32[]{:S(2)}) copy-start(f32[256,256]{1,0:T(8,128)} %param.10) | copy-start | bytes 786436
Sparse Core Ops, SparseCore 0:
  13.3 144.4 all-reduce.3
  161.7 87.7 all-reduce.5
where the time goes:
time: 265 us
  waiting for transfers between devices  165 us (62%)
  other arithmetic  56.8 us (21%)
  matrix products  19.4 us (7%)
  between operations  16.3 us (6%)
  local copies, waits for them, and re-layouts  6.65 us (3%)
    psum x1, waiting for transfers between devices, per_device(): lax.psum(jnp.dot(own_rows.T, own_rows, preferred_element_type=jnp.float32...  136 us
    another operation x6, other arithmetic, per_device(): factor_lower = jnp.linalg.cholesky(prior_gram + gram_data)  34 us
    psum x1, waiting for transfers between devices, per_device(): cross_data = lax.psum(cross_local, 'dp')  29.5 us
    another operation x4, other arithmetic, per_device(): lax.linalg.triangular_solve(factor_lower, cross, left_side=True, lower=True)  21.4 us
    dot_general x1, matrix products, row_product(): lax.dot_general(shared_block, panel_rows, (((0,), (0,)), ((), ())), prefe...  9.78 us
  transfers between devices with their start and end apart: 2, of which 2 were waited for; matrix products, arithmetic and copies ran while one was open for 27% of the time, Pallas kernels for 0%

commit v1 on v0

v1 whole, which is shorter than its diff:
```python
import jax
import jax.numpy as jnp
from jax import lax
from jax.experimental import pallas as pl
from jax.experimental.pallas import tpu as pltpu
from jax.sharding import PartitionSpec as P

ARCS = 32
F32 = jnp.float32
BF16 = jnp.bfloat16
HI = lax.Precision.HIGHEST
MESH = pl.DeviceIdType.MESH
SIDE = 4
PANEL = 256
CHUNK = 256
GROUP = PANEL // SIDE
HALF = PANEL // 2


def factor_block(a):
    n = a.shape[0]
    lane = lax.broadcasted_iota(jnp.int32, (n, n), 1)
    row = lax.broadcasted_iota(jnp.int32, (n, n), 0)
    z = jnp.concatenate([a, (lane == row).astype(F32)], axis=1)
    sub = lax.broadcasted_iota(jnp.int32, (8, 2 * n), 0)
    done = []
    for k in range(n // 8):
        m = n - 8 * k
        cols = [jnp.broadcast_to(z[:, 8 * k + j : 8 * k + j + 1], (m, 2 * n)) for j in range(8)]
        rows = lax.broadcasted_iota(jnp.int32, (m, 2 * n), 0)
        pivots = jnp.zeros((8, 2 * n), F32)
        for j in range(8):
            pivot = jnp.broadcast_to(cols[j][j : j + 1, :], (8, 2 * n))
            inverse = 1.0 / pivot
            pivots = jnp.where(sub == j, pivot, pivots)
            scale = jnp.where(rows > j, cols[j] * jnp.broadcast_to(inverse[0:1], (m, 2 * n)), 0.0)
            for i in range(j + 1, 8):
                cols[i] = cols[i] - scale * jnp.broadcast_to(cols[i][j : j + 1, :], (m, 2 * n))
            z = z - scale * jnp.broadcast_to(z[j : j + 1, :], (m, 2 * n))
        done.append(z[:8] * lax.rsqrt(pivots))
        z = z[8:]
    return jnp.concatenate(done, axis=0)


def factor_step(k, z_ref, upper_ref, inverse_ref):
    low, high = 64 * k, 64 * k + 64
    both = factor_block(z_ref[low:high, low:high])
    v = both[:, 64:]
    t = jnp.dot(v, z_ref[low:high, :], precision=HI, preferred_element_type=F32)
    lane = lax.broadcasted_iota(jnp.int32, (64, PANEL), 1)
    row = lax.broadcasted_iota(jnp.int32, (64, PANEL), 0)
    upper_ref[low:high, :] = jnp.where(lane >= low + row, t, 0.0)
    parts = [t[:, :low]] if k else []
    parts.append(v)
    if high < PANEL:
        parts.append(jnp.zeros((64, PANEL - high), F32))
    inverse = jnp.concatenate(parts, axis=1) if len(parts) > 1 else v
    inverse_ref[low:high, :] = inverse
    if high < PANEL:
        update = lax.dot_general(
            t[:, high:],
            jnp.where(lane < high, inverse, t),
            (((0,), (0,)), ((), ())),
            precision=HI,
            preferred_element_type=F32,
        )
        lane = lax.broadcasted_iota(jnp.int32, (PANEL - high, PANEL), 1)
        old = jnp.where((lane >= low) & (lane < high), 0.0, z_ref[high:, :])
        z_ref[high:, :] = old - update


def split2(a):
    first = a.astype(BF16)
    return first, (a - first.astype(F32)).astype(BF16)


def kernel(
    coef_hbm, arcs_hbm, live_ref, shared_hbm, prior_hbm, prior_shared_hbm,
    upper_hbm, out_hbm,
    coef, arcs, prior, prior_cols, panel, shared, prod, opp_in, side_in, total, group_in,
    full, out, gram_part, gram_in, gram_full, z, upper, inverse,
    small_sem, shared_sem, out_sem,
    opp_send, opp_recv, side_send, side_recv, group_send, group_recv,
    gs_send, gs_recv, gp_send, gp_recv, gf_send, gf_recv,
    g1_send, g1_recv, g2_send, g2_recv, g3_send, g3_recv,
):
    dp, col = lax.axis_index("dp"), lax.axis_index("col")
    x, z_at = dp // SIDE, dp % SIDE
    y, core = col // 2, col % 2

    def device(dx=0, dz=0, dy=0, dc=0):
        return (
            (x + dx) % SIDE * SIDE + (z_at + dz) % SIDE,
            (y + dy) % SIDE * 2 + (core + dc) % 2,
        )

    def along(half, d):
        return device(dx=d) if half == 0 else device(dz=d)

    def across(half, d):
        return device(dz=d) if half == 0 else device(dx=d)

    first_at = (x, z_at)
    second_at = (z_at, x)

    barrier = pltpu.get_barrier_semaphore()
    for d in (1, 2, 3):
        pl.semaphore_signal(barrier, inc=1, device_id=device(dx=d), device_id_type=MESH)
        pl.semaphore_signal(barrier, inc=1, device_id=device(dz=d), device_id_type=MESH)
    for dy in range(SIDE):
        for dc in range(2):
            if dy or dc:
                pl.semaphore_signal(
                    barrier, inc=1, device_id=device(dy=dy, dc=dc), device_id_type=MESH
                )

    loads = [
        pltpu.make_async_copy(arcs_hbm, arcs, small_sem.at[0]),
        pltpu.make_async_copy(coef_hbm, coef, small_sem.at[1]),
        pltpu.make_async_copy(prior_hbm, prior, small_sem.at[2]),
    ]
    for half in range(2):
        start = pl.multiple_of((half * SIDE + first_at[half]) * CHUNK, CHUNK)
        loads.append(
            pltpu.make_async_copy(
                prior_shared_hbm.at[:, pl.ds(start, CHUNK)],
                prior_cols.at[half],
                small_sem.at[3 + half],
            )
        )
    order = [(half, rel) for rel in (2, 1, 3, 0) for half in range(2)]
    shared_loads = []
    for half, rel in order:
        start = pl.multiple_of((half * SIDE + (first_at[half] + rel) % SIDE) * CHUNK, CHUNK)
        shared_loads.append(
            pltpu.make_async_copy(
                shared_hbm.at[:, pl.ds(start, CHUNK)],
                shared.at[half * SIDE + rel],
                shared_sem.at[half * SIDE + rel],
            )
        )
    loads[0].start()
    loads[1].start()
    shared_loads[0].start()
    shared_loads[1].start()
    shared_loads[2].start()

    rows = arcs.shape[1]
    loads[0].wait()
    loads[1].wait()
    live = live_ref[0]
    step = 512

    def build(i, carry):
        at = pl.ds(pl.multiple_of(i * step, step), step)
        pair = arcs[:, at]
        row = i * step + lax.broadcasted_iota(jnp.int32, (8, step), 1)
        inside = row < live
        one = jnp.where(inside, jnp.broadcast_to(pair[0:1], (8, step)), -1)
        two = jnp.where(inside, jnp.broadcast_to(pair[1:2], (8, step)), -1)
        values = coef[:, at].astype(F32)
        upper_values, lower_values = values[:8], values[8:]
        for a in range(0, ARCS, 2):
            tiles = [
                jnp.where(one == b, upper_values, jnp.where(two == b, lower_values, 0.0))
                for b in (a, a + 1)
            ]
            panel[8 * a : 8 * a + 16, at] = jnp.concatenate(tiles, axis=0).astype(BF16)
        return carry

    lax.fori_loop(0, rows // step, build, 0)

    own_rows = pl.ds(pl.multiple_of(col * 32, 32), 32)
    gram_part[0] = lax.dot_general(
        panel[own_rows, :],
        panel[...],
        (((1,), (1,)), ((), ())),
        preferred_element_type=F32,
    )
    pl.semaphore_wait(barrier, 13)

    def remote(src, dst, send, recv, to):
        return pltpu.make_async_remote_copy(
            src_ref=src, dst_ref=dst, send_sem=send, recv_sem=recv, device_id=to, device_id_type=MESH
        )

    def gram_axis(d, second):
        if second:
            return device(dx=d * core, dz=d * (1 - core))
        return device(dx=d * (1 - core), dz=d * core)

    g1 = [
        remote(gram_part.at[0], gram_in.at[d - 1], g1_send.at[d - 1], g1_recv.at[d - 1], gram_axis(d, False))
        for d in (1, 2, 3)
    ]
    g2 = [
        remote(gram_part.at[1], gram_in.at[2 + d], g2_send.at[d - 1], g2_recv.at[d - 1], gram_axis(d, True))
        for d in (1, 2, 3)
    ]
    g3 = []
    for dy in range(SIDE):
        for dc in range(2):
            if dy or dc:
                i = 2 * dy + dc - 1
                g3.append(
                    remote(
                        gram_part.at[2], gram_full.at[own_rows, :], g3_send.at[i], g3_recv.at[i],
                        device(dy=dy, dc=dc),
                    )
                )
    for copy in g1:
        copy.start()

    top, bottom = pl.ds(0, HALF), pl.ds(HALF, HALF)

    def opp_copy(half, side):
        where = top if side == 0 else bottom
        i = 2 * half + side
        return remote(
            prod.at[half * SIDE + 2, where, :], opp_in.at[i], opp_send.at[i], opp_recv.at[i],
            along(half, 1 if side == 0 else 3),
        )

    def side_copy(half, side, part):
        where = top if part == 0 else bottom
        i = 4 * half + 2 * side + part
        return remote(
            prod.at[half * SIDE + (1 if side == 0 else 3), where, :],
            side_in.at[2 * half + side, where, :],
            side_send.at[i], side_recv.at[i],
            along(half, 1 if side == 0 else 3),
        )

    def multiply(i):
        half, rel = order[i]
        at = half * SIDE + rel
        shared_loads[i].wait()
        prod[at] = jnp.dot(panel[...], shared[at], preferred_element_type=F32)

    for i in range(8):
        if i + 3 < 8:
            shared_loads[i + 3].start()
        multiply(i)
        half, rel = order[i]
        if rel == 2:
            opp_copy(half, 0).start()
            opp_copy(half, 1).start()
        elif rel == 1:
            side_copy(half, 0, 1).start()
        elif rel == 3:
            side_copy(half, 1, 0).start()
        if i == 3:
            for load in loads[2:]:
                load.start()
        if i == 5:
            for copy in g1:
                copy.wait_recv()
            gram_part[1] = gram_part[0] + gram_in[0] + gram_in[1] + gram_in[2]
            for copy in g2:
                copy.start()

    for side in range(2):
        for half in range(2):
            opp_copy(half, side).wait_recv()
            at = half * SIDE + (1 if side == 0 else 3)
            where = top if side == 0 else bottom
            prod[at, where, :] += opp_in[2 * half + side]
            side_copy(half, side, side).start()

    for load in loads[2:]:
        load.wait()
    prior_t = prior[...].T
    upper[...] = prior_t
    for half in range(2):
        group = pl.ds(pl.multiple_of(second_at[half] * GROUP, GROUP), GROUP)
        full[half * SIDE + first_at[half], group, :] = jnp.dot(
            upper[group, :], prior_cols[half], precision=HI, preferred_element_type=F32
        )
    z[...] = jnp.dot(prior_t, prior[...], precision=HI, preferred_element_type=F32)

    for copy in g2:
        copy.wait_recv()
    gram_part[2] = gram_part[1] + gram_in[3] + gram_in[4] + gram_in[5]
    for copy in g3:
        copy.start()
    gram_full[own_rows, :] = gram_part[2]

    def group_copy(half, d):
        i = 3 * half + d - 1
        group = pl.ds(pl.multiple_of((second_at[half] + d) % SIDE * GROUP, GROUP), GROUP)
        return remote(
            total.at[half, group, :], group_in.at[i], group_send.at[i], group_recv.at[i],
            across(half, d),
        )

    for half in range(2):
        for part in range(2):
            where = top if part == 0 else bottom
            side_copy(half, 0, part).wait_recv()
            side_copy(half, 1, part).wait_recv()
            total[half, where, :] = (
                prod[half * SIDE, where, :]
                + side_in[2 * half, where, :]
                + side_in[2 * half + 1, where, :]
            )
        for d in (2, 1, 3):
            group_copy(half, d).start()

    for copy in g3:
        copy.wait_recv()
    z[...] += gram_full[...]
    factor_step(0, z, upper, inverse)

    def own_copy(half, d):
        i = 3 * half + d - 1
        here = full.at[
            half * SIDE + first_at[half],
            pl.ds(pl.multiple_of(second_at[half] * GROUP, GROUP), GROUP),
            :,
        ]
        return remote(here, here, gs_send.at[i], gs_recv.at[i], across(half, d))

    def chunk_copy(half, d, side):
        i = 8 * half + 2 * d + side
        here = full.at[
            half * SIDE + first_at[half],
            pl.ds(pl.multiple_of((second_at[half] + SIDE - d) % SIDE * GROUP, GROUP), GROUP),
            :,
        ]
        return remote(here, here, gp_send.at[i], gp_recv.at[i], along(half, 1 if side == 0 else 3))

    def forward_copy(half, d, side):
        i = 8 * half + 2 * d + side
        start = (second_at[half] + SIDE - d) % SIDE * GROUP + side * (GROUP // 2)
        here = full.at[
            half * SIDE + (first_at[half] + (3 if side == 0 else 1)) % SIDE,
            pl.ds(pl.multiple_of(start, GROUP // 2), GROUP // 2),
            :,
        ]
        return remote(here, here, gf_send.at[i], gf_recv.at[i], along(half, 1 if side == 0 else 3))

    for half in range(2):
        group = pl.ds(pl.multiple_of(second_at[half] * GROUP, GROUP), GROUP)
        for d in (1, 2, 3):
            group_copy(half, d).wait_recv()
        full[half * SIDE + first_at[half], group, :] += (
            total[half, group, :]
            + group_in[3 * half]
            + group_in[3 * half + 1]
            + group_in[3 * half + 2]
        )
        for d in (2, 1, 3):
            own_copy(half, d).start()
        chunk_copy(half, 0, 0).start()
        chunk_copy(half, 0, 1).start()

    factor_step(1, z, upper, inverse)
    for d in (1, 3, 2):
        for half in range(2):
            own_copy(half, d).wait_recv()
            chunk_copy(half, d, 0).start()
            chunk_copy(half, d, 1).start()
    for half in range(2):
        for side in range(2):
            chunk_copy(half, 0, side).wait_recv()
            forward_copy(half, 0, side).start()
    factor_step(2, z, upper, inverse)
    for d in (1, 3, 2):
        for half in range(2):
            for side in range(2):
                chunk_copy(half, d, side).wait_recv()
                forward_copy(half, d, side).start()
    factor_step(3, z, upper, inverse)
    upper_copy = pltpu.make_async_copy(upper, upper_hbm, out_sem.at[8])
    upper_copy.start()

    w1, w2 = split2(inverse[...])
    weights = jnp.concatenate([w1, w1, w2], axis=1)

    def apply(half, rel):
        at = half * SIDE + (first_at[half] + rel) % SIDE
        a1, a2 = split2(full[at])
        out[half * SIDE + rel] = jnp.dot(
            weights, jnp.concatenate([a1, a2, a1], axis=0), preferred_element_type=F32
        )
        pltpu.make_async_copy(
            out.at[half * SIDE + rel],
            out_hbm.at[:, pl.ds(pl.multiple_of(at * CHUNK, CHUNK), CHUNK)],
            out_sem.at[half * SIDE + rel],
        ).start()

    for rel in (0, 1, 3):
        for half in range(2):
            apply(half, rel)
    for half in range(2):
        for d in range(SIDE):
            for side in range(2):
                forward_copy(half, d, side).wait_recv()
        apply(half, 2)

    for copy in g1 + g2 + g3:
        copy.wait_send()
    for half in range(2):
        for side in range(2):
            opp_copy(half, side).wait_send()
            for part in range(2):
                side_copy(half, side, part).wait_send()
            for d in range(SIDE):
                chunk_copy(half, d, side).wait_send()
                forward_copy(half, d, side).wait_send()
        for d in (1, 2, 3):
            group_copy(half, d).wait_send()
            own_copy(half, d).wait_send()
    upper_copy.wait()
    for half in range(2):
        for rel in range(SIDE):
            at = half * SIDE + (first_at[half] + rel) % SIDE
            pltpu.make_async_copy(
                out.at[half * SIDE + rel],
                out_hbm.at[:, pl.ds(pl.multiple_of(at * CHUNK, CHUNK), CHUNK)],
                out_sem.at[half * SIDE + rel],
            ).wait()


def per_device(coefficients, arc_pairs, live_rows, shared_rows, prior_panel, prior_shared):
    rows, columns = shared_rows.shape
    anywhere = pl.BlockSpec(memory_space=pl.ANY)
    dma = pltpu.SemaphoreType.DMA
    return pl.pallas_call(
        kernel,
        out_shape=[
            jax.ShapeDtypeStruct((PANEL, PANEL), F32),
            jax.ShapeDtypeStruct((PANEL, columns), F32),
        ],
        in_specs=[anywhere, anywhere, pl.BlockSpec(memory_space=pltpu.SMEM)] + [anywhere] * 3,
        out_specs=[anywhere, anywhere],
        scratch_shapes=[
            pltpu.VMEM(coefficients.shape, BF16),
            pltpu.VMEM(arc_pairs.shape, jnp.int32),
            pltpu.VMEM((PANEL, PANEL), F32),
            pltpu.VMEM((2, PANEL, CHUNK), F32),
            pltpu.VMEM((PANEL, rows), BF16),
            pltpu.VMEM((8, rows, CHUNK), BF16),
            pltpu.VMEM((8, PANEL, CHUNK), F32),
            pltpu.VMEM((4, HALF, CHUNK), F32),
            pltpu.VMEM((4, PANEL, CHUNK), F32),
            pltpu.VMEM((2, PANEL, CHUNK), F32),
            pltpu.VMEM((6, GROUP, CHUNK), F32),
            pltpu.VMEM((8, PANEL, CHUNK), F32),
            pltpu.VMEM((8, PANEL, CHUNK), F32),
            pltpu.VMEM((3, 32, PANEL), F32),
            pltpu.VMEM((6, 32, PANEL), F32),
            pltpu.VMEM((PANEL, PANEL), F32),
            pltpu.VMEM((PANEL, PANEL), F32),
            pltpu.VMEM((PANEL, PANEL), F32),
            pltpu.VMEM((PANEL, PANEL), F32),
            dma((5,)), dma((8,)), dma((9,)),
            dma((4,)), dma((4,)), dma((8,)), dma((8,)), dma((6,)), dma((6,)),
            dma((6,)), dma((6,)), dma((16,)), dma((16,)), dma((16,)), dma((16,)),
            dma((3,)), dma((3,)), dma((3,)), dma((3,)), dma((7,)), dma((7,)),
        ],
        compiler_params=pltpu.CompilerParams(
            collective_id=0, has_side_effects=True, vmem_limit_bytes=56 << 20
        ),
    )(coefficients, arc_pairs, live_rows, shared_rows, prior_panel, prior_shared)


def solution(mesh):
    in_specs = (P(None, "dp"), P(None, "dp"), P("dp"), P("dp", "col"), P(), P(None, "col"))
    out_specs = (P(), P(None, "col"))
    return jax.shard_map(
        per_device, mesh=mesh, in_specs=in_specs, out_specs=out_specs, check_vma=False
    )
```

time: 265 us -> 58.5 us (0.22)
  waiting for transfers between devices: 165 us -> 0 us
  other arithmetic: 56.8 us -> 0 us
  Pallas kernels: 0 us -> 52.3 us
  matrix products: 19.4 us -> 0 us
  between operations: 16.3 us -> 1.28 us
    psum x2 -> x0, waiting for transfers between devices: 165 us -> none  [the longest x1 136 us: per_device(): lax.psum(jnp.dot(own_rows.T, own_rows, preferred_element_type=jnp.float32...]
    another operation x10 -> x0, other arithmetic: 55.4 us -> none  [the longest x6 34 us: per_device(): factor_lower = jnp.linalg.cholesky(prior_gram + gram_data)]
    pallas_call x0 -> x1, Pallas kernels: none -> 52.3 us  [per_device(): pl.pallas_call(kernel, out_shape=[jax.ShapeDtypeStruct((PANEL, PANEL), F3...]
    dot_general x4 -> x0, matrix products: 15.8 us -> none  [the longest x1 9.78 us: row_product(): lax.dot_general(shared_block, panel_rows, (((0,), (0,)), ((), ())), prefe...]
    unnamed x5 -> x2, local copies, waits for them, and re-layouts: 0.85 us -> 4.8 us
    another operation x9 -> x0, local copies, waits for them, and re-layouts: 3.92 us -> none
    another operation x5 -> x0, matrix products: 3.62 us -> none  [the longest x3 3.15 us: per_device(): lax.linalg.triangular_solve(factor_lower, cross, left_side=True, lower=True)]
  transfers between devices with their start and end apart: 2 -> 0, of which waited for: 2 -> 0; matrix products, arithmetic and copies ran while one was open for 27% -> 0% of each run, Pallas kernels for 0% -> 0%
where the time goes in v1:
time: 58.5 us; the launch traced here: 58.4 us
  Pallas kernels  52.3 us (89%)
  local copies, waits for them, and re-layouts  4.8 us (8%)
  between operations  1.28 us (2%)
    pallas_call x1, Pallas kernels, per_device(): pl.pallas_call(kernel, out_shape=[jax.ShapeDtypeStruct((PANEL, PANEL), F3...  52.3 us
    unnamed x2, local copies, waits for them, and re-layouts  4.8 us

profile of v1, /device:TPU:0, one launch (start us, length us, event | category | flops | bytes accessed | tf_op | source)
XLA Modules:
  0.0 58.4 jit_solution(9657819145033513374)
XLA Ops:
  1.3 52.3 %shard_map.77 = (f32[256,256]{1,0:T(8,128)}, f32[256,2048]{1,0:T(8,128)}) custom-call(bf16[16,4096]{1,0:T(8,128)(2,1)} %coef_hbm.1, s32[2,4096]{1,0:T(2,128)} %arcs_hbm.1, s32[1]{0:T(128)S(6)} %copy.10.live_ref, bf16[4096,2048]{1,0:T(8,128)(2,1)} %shared_hbm.1, f32[256,256]{1,0:T(8,128)} %prior_hbm.1, f32[256,2048]{1,0:T(8,128)} %prior_shared_hbm.1), custom_call_target="tpu_custom_call" | custom-call | tf_op jit(solution)/shard_map/pallas_call | solution.py:429
  53.6 1.7 %copy.11 = f32[256,256]{1,0:T(8,128)} copy(f32[256,256]{1,0:T(8,128)} %get-tuple-element.4) | data formatting | bytes 524288
  55.2 3.1 %copy.12 = f32[256,2048]{1,0:T(8,128)} copy(f32[256,2048]{1,0:T(8,128)} %get-tuple-element.5) | data formatting | bytes 4194304

commit v2 on v1

v2 whole, which is shorter than its diff:
```python
import jax
import jax.numpy as jnp
from jax import lax
from jax.experimental import pallas as pl
from jax.experimental.pallas import tpu as pltpu
from jax.sharding import PartitionSpec as P

ARCS = 32
F32 = jnp.float32
BF16 = jnp.bfloat16
HI = lax.Precision.HIGHEST
MESH = pl.DeviceIdType.MESH
SIDE = 4
PANEL = 256
CHUNK = 256
GROUP = PANEL // SIDE
HALF = PANEL // 2


def factor_pieces(z_ref, upper_ref, inverse_ref):
    n = 64
    sub = lax.broadcasted_iota(jnp.int32, (8, 2 * n), 0)
    for k in range(PANEL // n):
        low, high = n * k, n * k + n
        lane = lax.broadcasted_iota(jnp.int32, (n, n), 1)
        row = lax.broadcasted_iota(jnp.int32, (n, n), 0)
        z = jnp.concatenate([z_ref[low:high, low:high], (lane == row).astype(F32)], axis=1)
        done = []
        for b in range(n // 8):
            m = n - 8 * b
            cols = [jnp.broadcast_to(z[:, 8 * b + j : 8 * b + j + 1], (m, 2 * n)) for j in range(8)]
            rows = lax.broadcasted_iota(jnp.int32, (m, 2 * n), 0)
            pivots = jnp.zeros((8, 2 * n), F32)
            for j in range(8):
                pivot = jnp.broadcast_to(cols[j][j : j + 1, :], (8, 2 * n))
                inverse = 1.0 / pivot
                pivots = jnp.where(sub == j, pivot, pivots)
                scale = jnp.where(
                    rows > j, cols[j] * jnp.broadcast_to(inverse[0:1], (m, 2 * n)), 0.0
                )
                for i in range(j + 1, 8):
                    cols[i] = cols[i] - scale * jnp.broadcast_to(cols[i][j : j + 1, :], (m, 2 * n))
                z = z - scale * jnp.broadcast_to(z[j : j + 1, :], (m, 2 * n))
            done.append(z[:8] * lax.rsqrt(pivots))
            z = z[8:]
            if b % 2 and b < 7:
                yield
        v = jnp.concatenate(done, axis=0)[:, n:]
        t = jnp.dot(v, z_ref[low:high, :], precision=HI, preferred_element_type=F32)
        lane = lax.broadcasted_iota(jnp.int32, (n, PANEL), 1)
        row = lax.broadcasted_iota(jnp.int32, (n, PANEL), 0)
        upper_ref[low:high, :] = jnp.where(lane >= low + row, t, 0.0)
        parts = [t[:, :low]] if k else []
        parts.append(v)
        if high < PANEL:
            parts.append(jnp.zeros((n, PANEL - high), F32))
        inverse = jnp.concatenate(parts, axis=1)
        inverse_ref[low:high, :] = inverse
        yield
        if high < PANEL:
            update = lax.dot_general(
                t[:, high:],
                jnp.where(lane < high, inverse, t),
                (((0,), (0,)), ((), ())),
                precision=HI,
                preferred_element_type=F32,
            )
            lane = lax.broadcasted_iota(jnp.int32, (PANEL - high, PANEL), 1)
            old = jnp.where((lane >= low) & (lane < high), 0.0, z_ref[high:, :])
            z_ref[high:, :] = old - update
            yield


def split2(a):
    first = a.astype(BF16)
    return first, (a - first.astype(F32)).astype(BF16)


def kernel(
    coef_hbm, arcs_hbm, live_hbm, shared_hbm, prior_hbm, prior_shared_hbm,
    upper, inverse, full,
    coef, arcs, live, prior, prior_t, prior_cols, panel, shared, prod, opp_in, side_in, total, group_in,
    gram_part, gram_in, gram_full, z,
    small_sem, shared_sem,
    opp_send, opp_recv, side_send, side_recv, group_send, group_recv,
    gs_send, gs_recv, gp_send, gp_recv, gf_send, gf_recv,
    g1_send, g1_recv, g2_send, g2_recv, g3_send, g3_recv,
):
    dp, col = lax.axis_index("dp"), lax.axis_index("col")
    x, z_at = dp // SIDE, dp % SIDE
    y, core = col // 2, col % 2

    def device(dx=0, dz=0, dy=0, dc=0):
        return (
            (x + dx) % SIDE * SIDE + (z_at + dz) % SIDE,
            (y + dy) % SIDE * 2 + (core + dc) % 2,
        )

    def along(half, d):
        return device(dx=d) if half == 0 else device(dz=d)

    def across(half, d):
        return device(dz=d) if half == 0 else device(dx=d)

    first_at = (x, z_at)
    second_at = (z_at, x)

    barrier = pltpu.get_barrier_semaphore()
    for d in (1, 2, 3):
        pl.semaphore_signal(barrier, inc=1, device_id=device(dx=d), device_id_type=MESH)
        pl.semaphore_signal(barrier, inc=1, device_id=device(dz=d), device_id_type=MESH)
    for dy in range(SIDE):
        for dc in range(2):
            if dy or dc:
                pl.semaphore_signal(
                    barrier, inc=1, device_id=device(dy=dy, dc=dc), device_id_type=MESH
                )

    loads = [
        pltpu.make_async_copy(arcs_hbm, arcs, small_sem.at[0]),
        pltpu.make_async_copy(coef_hbm, coef, small_sem.at[1]),
        pltpu.make_async_copy(live_hbm, live, small_sem.at[2]),
        pltpu.make_async_copy(prior_hbm, prior, small_sem.at[3]),
    ]
    for half in range(2):
        start = pl.multiple_of((half * SIDE + first_at[half]) * CHUNK, CHUNK)
        loads.append(
            pltpu.make_async_copy(
                prior_shared_hbm.at[:, pl.ds(start, CHUNK)],
                prior_cols.at[half],
                small_sem.at[4 + half],
            )
        )
    order = [(half, rel) for rel in (2, 1, 3, 0) for half in range(2)]
    shared_loads = []
    for half, rel in order:
        start = pl.multiple_of((half * SIDE + (first_at[half] + rel) % SIDE) * CHUNK, CHUNK)
        shared_loads.append(
            pltpu.make_async_copy(
                shared_hbm.at[:, pl.ds(start, CHUNK)],
                shared.at[half * SIDE + rel],
                shared_sem.at[half * SIDE + rel],
            )
        )
    for load in loads[:3]:
        load.start()
    shared_loads[0].start()

    rows = arcs.shape[1]
    for load in loads[:3]:
        load.wait()
    live_count = live[0]
    shared_loads[1].start()
    step = 512

    def build(i, carry):
        at = pl.ds(pl.multiple_of(i * step, step), step)
        pair = arcs[:, at]
        row = i * step + lax.broadcasted_iota(jnp.int32, (8, step), 1)
        inside = row < live_count
        one = jnp.where(inside, jnp.broadcast_to(pair[0:1], (8, step)), -1)
        two = jnp.where(inside, jnp.broadcast_to(pair[1:2], (8, step)), -1)
        values = coef[:, at].astype(F32)
        upper_values, lower_values = values[:8], values[8:]
        for a in range(0, ARCS, 2):
            tiles = [
                jnp.where(one == b, upper_values, jnp.where(two == b, lower_values, 0.0))
                for b in (a, a + 1)
            ]
            panel[8 * a : 8 * a + 16, at] = jnp.concatenate(tiles, axis=0).astype(BF16)
        return carry

    lax.fori_loop(0, rows // step, build, 0)
    shared_loads[2].start()

    own_rows = pl.ds(pl.multiple_of(col * 32, 32), 32)

    def remote(src, dst, send, recv, to):
        return pltpu.make_async_remote_copy(
            src_ref=src, dst_ref=dst, send_sem=send, recv_sem=recv, device_id=to, device_id_type=MESH
        )

    def gram_axis(d, second):
        if second:
            return device(dx=d * core, dz=d * (1 - core))
        return device(dx=d * (1 - core), dz=d * core)

    g1 = [
        remote(gram_part.at[0], gram_in.at[d - 1], g1_send.at[d - 1], g1_recv.at[d - 1], gram_axis(d, False))
        for d in (1, 2, 3)
    ]
    g2 = [
        remote(gram_part.at[1], gram_in.at[2 + d], g2_send.at[d - 1], g2_recv.at[d - 1], gram_axis(d, True))
        for d in (1, 2, 3)
    ]
    g3 = []
    for dy in range(SIDE):
        for dc in range(2):
            if dy or dc:
                i = 2 * dy + dc - 1
                g3.append(
                    remote(
                        gram_part.at[2], gram_full.at[own_rows, :], g3_send.at[i], g3_recv.at[i],
                        device(dy=dy, dc=dc),
                    )
                )
    def rows_of(half, e):
        return pl.ds(pl.multiple_of((second_at[half] + e) % SIDE * GROUP, GROUP), GROUP)

    def opp_copy(half, side, e):
        i = 4 * half + 2 * side + (e in (1, 0))
        return remote(
            prod.at[half * SIDE + 2, rows_of(half, e), :],
            opp_in.at[i], opp_send.at[i], opp_recv.at[i],
            along(half, 1 if side == 0 else 3),
        )

    def side_copy(half, side, e):
        i = 8 * half + 4 * side + e
        return remote(
            prod.at[half * SIDE + (1 if side == 0 else 3), rows_of(half, e), :],
            side_in.at[2 * half + side, rows_of(half, e), :],
            side_send.at[i], side_recv.at[i],
            along(half, 1 if side == 0 else 3),
        )

    def multiply(i):
        half, rel = order[i]
        at = half * SIDE + rel
        shared_loads[i].wait()
        if i + 3 < 8:
            shared_loads[i + 3].start()
        prod[at] = jnp.dot(panel[...], shared[at], preferred_element_type=F32)

    def relay(half, side, e):
        opp_copy(half, side, e).wait_recv()
        prod[half * SIDE + (1 if side == 0 else 3), rows_of(half, e), :] += opp_in[
            4 * half + 2 * side + (e in (1, 0))
        ]
        side_copy(half, side, e).start()

    multiply(0)
    pl.semaphore_wait(barrier, 13)
    for half in range(2):
        if half:
            multiply(1)
        for side, e in ((0, 2), (1, 3), (0, 1), (1, 0)):
            opp_copy(half, side, e).start()
    gram_part[0] = lax.dot_general(
        panel[own_rows, :],
        panel[...],
        (((1,), (1,)), ((), ())),
        preferred_element_type=F32,
    )
    for copy in g1:
        copy.start()
    for i, side, e in ((2, 0, 3), (3, 0, 3), (4, 1, 2), (5, 1, 2)):
        multiply(i)
        side_copy(order[i][0], side, e).start()
    for load in loads[3:]:
        load.start()
    for copy in g1:
        copy.wait_recv()
    gram_part[1] = gram_part[0] + gram_in[0] + gram_in[1] + gram_in[2]
    for copy in g2:
        copy.start()

    for half in range(2):
        relay(half, 0, 2)
        relay(half, 1, 3)
    multiply(6)
    multiply(7)
    for half in range(2):
        relay(half, 0, 1)
        side_copy(half, 1, 1).start()
    for half in range(2):
        relay(half, 1, 0)
        side_copy(half, 0, 0).start()

    for copy in g2:
        copy.wait_recv()
    gram_part[2] = gram_part[1] + gram_in[3] + gram_in[4] + gram_in[5]
    for copy in g3:
        copy.start()
    gram_full[own_rows, :] = gram_part[2]

    def group_copy(half, e):
        i = 3 * half + e - 1
        return remote(
            total.at[half, rows_of(half, e), :], group_in.at[i], group_send.at[i], group_recv.at[i],
            across(half, e),
        )

    def finish(half, e):
        side_copy(half, 0, e).wait_recv()
        side_copy(half, 1, e).wait_recv()
        here = rows_of(half, e)
        total[half, here, :] = (
            prod[half * SIDE, here, :] + side_in[2 * half, here, :] + side_in[2 * half + 1, here, :]
        )
        if e:
            group_copy(half, e).start()

    for e in (2, 3):
        for half in range(2):
            finish(half, e)

    for load in loads[3:]:
        load.wait()
    prior_t[...] = prior[...].T
    for half in range(2):
        own = rows_of(half, 0)
        full[half * SIDE + first_at[half], own, :] = jnp.dot(
            prior_t[own, :], prior_cols[half], precision=HI, preferred_element_type=F32
        )
    for e in (1, 0):
        for half in range(2):
            finish(half, e)
    z[...] = jnp.dot(prior_t[...], prior[...], precision=HI, preferred_element_type=F32)

    def own_copy(half, d):
        i = 3 * half + d - 1
        here = full.at[half * SIDE + first_at[half], rows_of(half, 0), :]
        return remote(here, here, gs_send.at[i], gs_recv.at[i], across(half, d))

    def chunk_copy(half, d, side):
        i = 8 * half + 2 * d + side
        here = full.at[half * SIDE + first_at[half], rows_of(half, SIDE - d), :]
        return remote(here, here, gp_send.at[i], gp_recv.at[i], along(half, 1 if side == 0 else 3))

    def forward_copy(half, d, side):
        i = 8 * half + 2 * d + side
        start = (second_at[half] + SIDE - d) % SIDE * GROUP + side * (GROUP // 2)
        here = full.at[
            half * SIDE + (first_at[half] + (3 if side == 0 else 1)) % SIDE,
            pl.ds(pl.multiple_of(start, GROUP // 2), GROUP // 2),
            :,
        ]
        return remote(here, here, gf_send.at[i], gf_recv.at[i], along(half, 1 if side == 0 else 3))

    for half in range(2):
        for e in (3, 1, 2):
            group_copy(half, e).wait_recv()
        own = rows_of(half, 0)
        full[half * SIDE + first_at[half], own, :] += (
            total[half, own, :]
            + group_in[3 * half]
            + group_in[3 * half + 1]
            + group_in[3 * half + 2]
        )
        for d in (2, 1, 3):
            own_copy(half, d).start()
    for half in range(2):
        chunk_copy(half, 0, 0).start()
        chunk_copy(half, 0, 1).start()

    for copy in g3:
        copy.wait_recv()
    z[...] += gram_full[...]
    pieces = factor_pieces(z, upper, inverse)

    def advance(count):
        for _ in range(count):
            next(pieces, None)

    advance(8)
    for d in (1, 3):
        for half in range(2):
            own_copy(half, d).wait_recv()
            chunk_copy(half, d, 0).start()
            chunk_copy(half, d, 1).start()
    advance(3)
    for half in range(2):
        own_copy(half, 2).wait_recv()
        chunk_copy(half, 2, 0).start()
        chunk_copy(half, 2, 1).start()
    for d in (0, 1, 3, 2):
        advance(3)
        for half in range(2):
            for side in range(2):
                chunk_copy(half, d, side).wait_recv()
                forward_copy(half, d, side).start()
    for _ in pieces:
        pass

    for d in (0, 1, 3, 2):
        for half in range(2):
            for side in range(2):
                forward_copy(half, d, side).wait_recv()

    for copy in g1 + g2 + g3:
        copy.wait_send()
    for half in range(2):
        for side, e in ((0, 2), (1, 3), (0, 1), (1, 0)):
            opp_copy(half, side, e).wait_send()
        for side in range(2):
            for e in range(SIDE):
                side_copy(half, side, e).wait_send()
                chunk_copy(half, e, side).wait_send()
                forward_copy(half, e, side).wait_send()
        for d in (1, 2, 3):
            group_copy(half, d).wait_send()
            own_copy(half, d).wait_send()


def apply_kernel(upper, inverse, full, upper_hbm, out_hbm, out, sem):
    upper_copy = pltpu.make_async_copy(upper, upper_hbm, sem.at[8])
    upper_copy.start()
    w1, w2 = split2(inverse[...])
    weights = jnp.concatenate([w1, w1, w2], axis=1)
    copies = []
    for i in range(8):
        a1, a2 = split2(full[i])
        out[i] = jnp.dot(
            weights, jnp.concatenate([a1, a2, a1], axis=0), preferred_element_type=F32
        )
        copies.append(
            pltpu.make_async_copy(out.at[i], out_hbm.at[:, pl.ds(i * CHUNK, CHUNK)], sem.at[i])
        )
        copies[-1].start()
    upper_copy.wait()
    for copy in copies:
        copy.wait()


def per_device(coefficients, arc_pairs, live_rows, shared_rows, prior_panel, prior_shared):
    rows, columns = shared_rows.shape
    hbm = pl.BlockSpec(memory_space=pltpu.HBM)
    vmem = pl.BlockSpec(memory_space=pltpu.VMEM)
    dma = pltpu.SemaphoreType.DMA
    upper, inverse, full = pl.pallas_call(
        kernel,
        out_shape=[
            pltpu.VMEM((PANEL, PANEL), F32),
            pltpu.VMEM((PANEL, PANEL), F32),
            pltpu.VMEM((8, PANEL, CHUNK), F32),
        ],
        in_specs=[hbm] * 6,
        out_specs=[vmem] * 3,
        scratch_shapes=[
            pltpu.VMEM(coefficients.shape, BF16),
            pltpu.VMEM(arc_pairs.shape, jnp.int32),
            pltpu.SMEM(live_rows.shape, jnp.int32),
            pltpu.VMEM((PANEL, PANEL), F32),
            pltpu.VMEM((PANEL, PANEL), F32),
            pltpu.VMEM((2, PANEL, CHUNK), F32),
            pltpu.VMEM((PANEL, rows), BF16),
            pltpu.VMEM((8, rows, CHUNK), BF16),
            pltpu.VMEM((8, PANEL, CHUNK), F32),
            pltpu.VMEM((8, GROUP, CHUNK), F32),
            pltpu.VMEM((4, PANEL, CHUNK), F32),
            pltpu.VMEM((2, PANEL, CHUNK), F32),
            pltpu.VMEM((6, GROUP, CHUNK), F32),
            pltpu.VMEM((3, 32, PANEL), F32),
            pltpu.VMEM((6, 32, PANEL), F32),
            pltpu.VMEM((PANEL, PANEL), F32),
            pltpu.VMEM((PANEL, PANEL), F32),
            dma((6,)), dma((8,)),
            dma((8,)), dma((8,)), dma((16,)), dma((16,)), dma((6,)), dma((6,)),
            dma((6,)), dma((6,)), dma((16,)), dma((16,)), dma((16,)), dma((16,)),
            dma((3,)), dma((3,)), dma((3,)), dma((3,)), dma((7,)), dma((7,)),
        ],
        compiler_params=pltpu.CompilerParams(
            collective_id=0, has_side_effects=True, vmem_limit_bytes=60 << 20
        ),
    )(coefficients, arc_pairs, live_rows, shared_rows, prior_panel, prior_shared)
    return pl.pallas_call(
        apply_kernel,
        out_shape=[
            jax.ShapeDtypeStruct((PANEL, PANEL), F32),
            jax.ShapeDtypeStruct((PANEL, columns), F32),
        ],
        in_specs=[vmem] * 3,
        out_specs=[hbm] * 2,
        scratch_shapes=[pltpu.VMEM((8, PANEL, CHUNK), F32), dma((9,))],
        compiler_params=pltpu.CompilerParams(vmem_limit_bytes=16 << 20),
    )(upper, inverse, full)


def solution(mesh):
    in_specs = (P(None, "dp"), P(None, "dp"), P("dp"), P("dp", "col"), P(), P(None, "col"))
    out_specs = (P(), P(None, "col"))
    return jax.shard_map(
        per_device, mesh=mesh, in_specs=in_specs, out_specs=out_specs, check_vma=False
    )
```

time: 58.5 us -> 45.8 us (0.78)
  Pallas kernels: 52.3 us -> 44.4 us
  local copies, waits for them, and re-layouts: 4.8 us -> 0 us
    pallas_call x1 -> x2, Pallas kernels: 52.3 us -> 44.4 us  [the longest x1 42.4 us: per_device(): pl.pallas_call(kernel, out_shape=[pltpu.VMEM((PANEL, PANEL), F32), pltpu....]
    unnamed x2 -> x0, local copies, waits for them, and re-layouts: 4.8 us -> none
where the time goes in v2:
time: 45.8 us; the launch traced here: 45.6 us
  Pallas kernels  44.4 us (97%)
  between operations  1.28 us (3%)
    pallas_call x1, Pallas kernels, per_device(): pl.pallas_call(kernel, out_shape=[pltpu.VMEM((PANEL, PANEL), F32), pltpu....  42.4 us
    pallas_call x1, Pallas kernels, per_device(): pl.pallas_call(apply_kernel, out_shape=[jax.ShapeDtypeStruct((PANEL, PANE...  1.93 us

profile of v2, /device:TPU:0, one launch (start us, length us, event | category | flops | bytes accessed | tf_op | source)
XLA Modules:
  0.0 45.6 jit_solution(12316863149670876979)
XLA Ops:
  1.3 42.4 %shard_map.77 = (f32[256,256]{1,0:T(8,128)S(1)}, f32[256,256]{1,0:T(8,128)S(1)}, f32[8,256,256]{2,1,0:T(8,128)S(1)}) custom-call(bf16[16,4096]{1,0:T(8,128)(2,1)} %coef_hbm.1, s32[2,4096]{1,0:T(2,128)} %arcs_hbm.1, s32[1]{0:T(128)S(6)} %copy.8.live_hbm, bf16[4096,2048]{1,0:T(8,128)(2,1)} %shared_hbm.1, f32[256,256]{1,0:T(8,128)} %prior_hbm.1, ...), custom_call_target="tpu_custom_call" | custom-call | tf_op jit(solution)/shard_map/pallas_call | solution.py:431
  43.7 1.9 %shard_map.78 = (f32[256,256]{1,0:T(8,128)}, f32[256,2048]{1,0:T(8,128)}) custom-call(f32[256,256]{1,0:T(8,128)S(1)} %get-tuple-element.5.upper, f32[256,256]{1,0:T(8,128)S(1)} %get-tuple-element.6.inverse, f32[8,256,256]{2,1,0:T(8,128)S(1)} %get-tuple-element.7.full), custom_call_target="tpu_custom_call" | custom-call | tf_op jit(solution)/shard_map/pallas_call | solution.py:467

commit v3 on v2

--- a/solution.py
+++ b/solution.py
@@ -15,6 +15,23 @@
 CHUNK = 256
 GROUP = PANEL // SIDE
 HALF = PANEL // 2
+
+
+def split3(a):
+    first = a.astype(BF16)
+    rest = a - first.astype(F32)
+    second = rest.astype(BF16)
+    return first, second, (rest - second.astype(F32)).astype(BF16)
+
+
+def product(x, y):
+    x1, x2, x3 = split3(x)
+    y1, y2, y3 = split3(y)
+    return jnp.dot(
+        jnp.concatenate([x1, x1, x2, x2, x1, x3], axis=1),
+        jnp.concatenate([y1, y2, y1, y2, y3, y1], axis=0),
+        preferred_element_type=F32,
+    )
 
 
 def factor_pieces(z_ref, upper_ref, inverse_ref):
@@ -46,7 +63,7 @@
             if b % 2 and b < 7:
                 yield
         v = jnp.concatenate(done, axis=0)[:, n:]
-        t = jnp.dot(v, z_ref[low:high, :], precision=HI, preferred_element_type=F32)
+        t = product(v, z_ref[low:high, :])
         lane = lax.broadcasted_iota(jnp.int32, (n, PANEL), 1)
         row = lax.broadcasted_iota(jnp.int32, (n, PANEL), 0)
         upper_ref[low:high, :] = jnp.where(lane >= low + row, t, 0.0)
@@ -58,13 +75,7 @@
         inverse_ref[low:high, :] = inverse
         yield
         if high < PANEL:
-            update = lax.dot_general(
-                t[:, high:],
-                jnp.where(lane < high, inverse, t),
-                (((0,), (0,)), ((), ())),
-                precision=HI,
-                preferred_element_type=F32,
-            )
+            update = product(t[:, high:].T, jnp.where(lane < high, inverse, t))
             lane = lax.broadcasted_iota(jnp.int32, (PANEL - high, PANEL), 1)
             old = jnp.where((lane >= low) & (lane < high), 0.0, z_ref[high:, :])
             z_ref[high:, :] = old - update
@@ -151,27 +162,29 @@
         load.wait()
     live_count = live[0]
     shared_loads[1].start()
+    shared_loads[2].start()
     step = 512
 
     def build(i, carry):
         at = pl.ds(pl.multiple_of(i * step, step), step)
         pair = arcs[:, at]
-        row = i * step + lax.broadcasted_iota(jnp.int32, (8, step), 1)
-        inside = row < live_count
-        one = jnp.where(inside, jnp.broadcast_to(pair[0:1], (8, step)), -1)
-        two = jnp.where(inside, jnp.broadcast_to(pair[1:2], (8, step)), -1)
-        values = coef[:, at].astype(F32)
-        upper_values, lower_values = values[:8], values[8:]
+        inside = i * step + lax.broadcasted_iota(jnp.int32, (1, step), 1) < live_count
+        pair = jnp.where(inside, pair, -1).astype(F32)
+        one = jnp.broadcast_to(pair[0:1], (16, step)).astype(BF16)
+        two = jnp.broadcast_to(pair[1:2], (16, step)).astype(BF16)
+        values = coef[:, at]
+        first_values = jnp.concatenate([values[:8], values[:8]], axis=0)
+        second_values = jnp.concatenate([values[8:], values[8:]], axis=0)
+        odd = (lax.broadcasted_iota(jnp.int32, (16, step), 0) // 8).astype(F32)
         for a in range(0, ARCS, 2):
-            tiles = [
-                jnp.where(one == b, upper_values, jnp.where(two == b, lower_values, 0.0))
-                for b in (a, a + 1)
-            ]
-            panel[8 * a : 8 * a + 16, at] = jnp.concatenate(tiles, axis=0).astype(BF16)
+            arc = (odd + a).astype(BF16)
+            panel[8 * a : 8 * a + 16, at] = jnp.where(
+                one == arc, first_values, jnp.where(two == arc, second_values, jnp.zeros((), BF16))
+            )
         return carry
 
     lax.fori_loop(0, rows // step, build, 0)
-    shared_loads[2].start()
+    shared_loads[3].start()
 
     own_rows = pl.ds(pl.multiple_of(col * 32, 32), 32)
 
@@ -228,8 +241,8 @@
         half, rel = order[i]
         at = half * SIDE + rel
         shared_loads[i].wait()
-        if i + 3 < 8:
-            shared_loads[i + 3].start()
+        if 4 <= i + 4 < 8:
+            shared_loads[i + 4].start()
         prod[at] = jnp.dot(panel[...], shared[at], preferred_element_type=F32)
 
     def relay(half, side, e):
@@ -239,32 +252,35 @@
         ]
         side_copy(half, side, e).start()
 
-    multiply(0)
-    pl.semaphore_wait(barrier, 13)
-    for half in range(2):
-        if half:
-            multiply(1)
-        for side, e in ((0, 2), (1, 3), (0, 1), (1, 0)):
-            opp_copy(half, side, e).start()
     gram_part[0] = lax.dot_general(
         panel[own_rows, :],
         panel[...],
         (((1,), (1,)), ((), ())),
         preferred_element_type=F32,
     )
+    multiply(0)
+    pl.semaphore_wait(barrier, 13)
     for copy in g1:
         copy.start()
+    for half in range(2):
+        if half:
+            multiply(1)
+        opp_copy(half, 0, 2).start()
+        opp_copy(half, 1, 3).start()
+    for half in range(2):
+        opp_copy(half, 0, 1).start()
+        opp_copy(half, 1, 0).start()
     for i, side, e in ((2, 0, 3), (3, 0, 3), (4, 1, 2), (5, 1, 2)):
         multiply(i)
         side_copy(order[i][0], side, e).start()
     for load in loads[3:]:
         load.start()
+
     for copy in g1:
         copy.wait_recv()
     gram_part[1] = gram_part[0] + gram_in[0] + gram_in[1] + gram_in[2]
     for copy in g2:
         copy.start()
-
     for half in range(2):
         relay(half, 0, 2)
         relay(half, 1, 3)
@@ -276,6 +292,36 @@
     for half in range(2):
         relay(half, 1, 0)
         side_copy(half, 0, 0).start()
+
+
+    for load in loads[3:]:
+        load.wait()
+    prior_t[...] = prior[...].T
+    for half in range(2):
+        own = rows_of(half, 0)
+        full[half * SIDE + first_at[half], own, :] = jnp.dot(
+            prior_t[own, :], prior_cols[half], precision=HI, preferred_element_type=F32
+        )
+    def group_copy(half, e):
+        i = 3 * half + e - 1
+        return remote(
+            total.at[half, rows_of(half, e), :], group_in.at[i], group_send.at[i], group_recv.at[i],
+            across(half, e),
+        )
+
+    def finish(half, e):
+        side_copy(half, 0, e).wait_recv()
+        side_copy(half, 1, e).wait_recv()
+        here = rows_of(half, e)
+        total[half, here, :] = (
+            prod[half * SIDE, here, :] + side_in[2 * half, here, :] + side_in[2 * half + 1, here, :]
+        )
+        if e:
+            group_copy(half, e).start()
+
+    for e in (2, 3):
+        for half in range(2):
+            finish(half, e)
 
     for copy in g2:
         copy.wait_recv()
@@ -283,39 +329,17 @@
     for copy in g3:
         copy.start()
     gram_full[own_rows, :] = gram_part[2]
-
-    def group_copy(half, e):
-        i = 3 * half + e - 1
-        return remote(
-            total.at[half, rows_of(half, e), :], group_in.at[i], group_send.at[i], group_recv.at[i],
-            across(half, e),
-        )
-
-    def finish(half, e):
-        side_copy(half, 0, e).wait_recv()
-        side_copy(half, 1, e).wait_recv()
-        here = rows_of(half, e)
-        total[half, here, :] = (
-            prod[half * SIDE, here, :] + side_in[2 * half, here, :] + side_in[2 * half + 1, here, :]
-        )
-        if e:
-            group_copy(half, e).start()
-
-    for e in (2, 3):
-        for half in range(2):
-            finish(half, e)
-
-    for load in loads[3:]:
-        load.wait()
-    prior_t[...] = prior[...].T
-    for half in range(2):
-        own = rows_of(half, 0)
-        full[half * SIDE + first_at[half], own, :] = jnp.dot(
-            prior_t[own, :], prior_cols[half], precision=HI, preferred_element_type=F32
-        )
     for e in (1, 0):
         for half in range(2):
             finish(half, e)
+    for copy in g1 + g2:
+        copy.wait_send()
+    for half in range(2):
+        for side, e in ((0, 2), (1, 3), (0, 1), (1, 0)):
+            opp_copy(half, side, e).wait_send()
+        for side in range(2):
+            for e in range(SIDE):
+                side_copy(half, side, e).wait_send()
     z[...] = jnp.dot(prior_t[...], prior[...], precision=HI, preferred_element_type=F32)
 
     def own_copy(half, d):
@@ -348,7 +372,7 @@
             + group_in[3 * half + 1]
             + group_in[3 * half + 2]
         )
-        for d in (2, 1, 3):
+        for d in (1, 3, 2):
             own_copy(half, d).start()
     for half in range(2):
         chunk_copy(half, 0, 0).start()
@@ -370,6 +394,11 @@
             chunk_copy(half, d, 0).start()
             chunk_copy(half, d, 1).start()
     advance(3)
+    for half in range(2):
+        for d in (1, 2, 3):
+            group_copy(half, d).wait_send()
+    for copy in g3:
+        copy.wait_send()
     for half in range(2):
         own_copy(half, 2).wait_recv()
         chunk_copy(half, 2, 0).start()
@@ -382,25 +411,23 @@
                 forward_copy(half, d, side).start()
     for _ in pieces:
         pass
+    for half in range(2):
+        for d in (1, 2, 3):
+            own_copy(half, d).wait_send()
+        for side in range(2):
+            for d in (0, 1, 3):
+                chunk_copy(half, d, side).wait_send()
 
     for d in (0, 1, 3, 2):
         for half in range(2):
             for side in range(2):
                 forward_copy(half, d, side).wait_recv()
 
-    for copy in g1 + g2 + g3:
-        copy.wait_send()
-    for half in range(2):
-        for side, e in ((0, 2), (1, 3), (0, 1), (1, 0)):
-            opp_copy(half, side, e).wait_send()
+    for half in range(2):
         for side in range(2):
-            for e in range(SIDE):
-                side_copy(half, side, e).wait_send()
-                chunk_copy(half, e, side).wait_send()
-                forward_copy(half, e, side).wait_send()
-        for d in (1, 2, 3):
-            group_copy(half, d).wait_send()
-            own_copy(half, d).wait_send()
+            for d in range(SIDE):
+                forward_copy(half, d, side).wait_send()
+            chunk_copy(half, 2, side).wait_send()
 
 
 def apply_kernel(upper, inverse, full, upper_hbm, out_hbm, out, sem):

time: 45.8 us -> 44.2 us (0.965)
  Pallas kernels: 44.4 us -> 42.6 us
    pallas_call x1, Pallas kernels: 42.4 us -> 40.7 us  [per_device(): pl.pallas_call(kernel, out_shape=[pltpu.VMEM((PANEL, PANEL), F32), pltpu....]
where the time goes in v3:
time: 44.2 us; the launch traced here: 43.9 us
  Pallas kernels  42.6 us (96%)
  between operations  1.28 us (3%)
    pallas_call x1, Pallas kernels, per_device(): pl.pallas_call(kernel, out_shape=[pltpu.VMEM((PANEL, PANEL), F32), pltpu....  40.7 us
    pallas_call x1, Pallas kernels, per_device(): pl.pallas_call(apply_kernel, out_shape=[jax.ShapeDtypeStruct((PANEL, PANE...  1.93 us

profile of v3, /device:TPU:0, one launch (start us, length us, event | category | flops | bytes accessed | tf_op | source)
XLA Modules:
  0.0 43.9 jit_solution(14849568919739474133)
XLA Ops:
  1.3 40.7 %shard_map.77 = (f32[256,256]{1,0:T(8,128)S(1)}, f32[256,256]{1,0:T(8,128)S(1)}, f32[8,256,256]{2,1,0:T(8,128)S(1)}) custom-call(bf16[16,4096]{1,0:T(8,128)(2,1)} %coef_hbm.1, s32[2,4096]{1,0:T(2,128)} %arcs_hbm.1, s32[1]{0:T(128)S(6)} %copy.8.live_hbm, bf16[4096,2048]{1,0:T(8,128)(2,1)} %shared_hbm.1, f32[256,256]{1,0:T(8,128)} %prior_hbm.1, ...), custom_call_target="tpu_custom_call" | custom-call | tf_op jit(solution)/shard_map/pallas_call | solution.py:458
  41.9 1.9 %shard_map.78 = (f32[256,256]{1,0:T(8,128)}, f32[256,2048]{1,0:T(8,128)}) custom-call(f32[256,256]{1,0:T(8,128)S(1)} %get-tuple-element.5.upper, f32[256,256]{1,0:T(8,128)S(1)} %get-tuple-element.6.inverse, f32[8,256,256]{2,1,0:T(8,128)S(1)} %get-tuple-element.7.full), custom_call_target="tpu_custom_call" | custom-call | tf_op jit(solution)/shard_map/pallas_call | solution.py:494
